TPU v7x, 512 devices: a whole 4x4x16 slice. The times are simulated.
512 devices in a mesh: row: 16 (over x, y), col: 32 (over z, core).
Axes of the slice: x: 4, y: 4, z: 16, core: 2. Of those that a mesh axis runs over, the one named last changes fastest.
Arguments:
- integrals: bfloat16 [512, 16, 6, 128, 128], P(('col', 'row')), may hold values from -0.21875 to 0.21875
- green_panel: bfloat16 [480, 2048], P('col'), may hold values from -6 to 6
- neighbours: int32 [16, 6], replicated, may hold values from 0 to 15, as said below
- slot_counts: int32 [16], replicated, may hold values from 1 to 6, as said below
Outputs:
- contracted: bfloat16 [512, 2048, 480], P('col', 'row')
Inputs may be any that keep to these rules, and one draw needn't show every extreme that they name: `neighbours`: atom indices. `slot_counts`: some atom uses all 6 slots.
All inputs are finite; a program needn't handle non-finite values.
Results may differ from a plain program's by a relative error of at most 0.001.
Values may be sent and summed in bfloat16 or wider, within the bound.
A program may use at most 64 MiB of HBM per device.

v0:
```python
import jax
import jax.numpy as jnp
from jax import lax
from jax.sharding import PartitionSpec as P


def per_device(integrals, green_panel, neighbours, slot_counts):
    atom_count = neighbours.shape[0]
    slot_count = neighbours.shape[1]
    block_width = integrals.shape[-1]
    keep_all = jnp.arange(slot_count, dtype=jnp.int32)[None, :] < slot_counts[:, None]
    regrouped = lax.all_to_all(integrals, "row", split_axis=1, concat_axis=0, tiled=True)
    local_atoms = regrouped.shape[1]
    first_atom = lax.axis_index("row") * local_atoms
    links_part = lax.dynamic_slice_in_dim(neighbours, first_atom, local_atoms, 0)
    keep_part = lax.dynamic_slice_in_dim(keep_all, first_atom, local_atoms, 0)
    local_atoms = regrouped.shape[1]
    whole_green = lax.all_gather(green_panel, "col", axis=0, tiled=True)
    panel_rows = whole_green.shape[0]
    spread = whole_green.reshape(panel_rows, atom_count, block_width)
    chosen = jnp.take(spread, links_part.reshape(-1), axis=1)
    chosen = chosen.reshape(panel_rows, local_atoms, slot_count, block_width)
    chosen = jnp.where(keep_part[None, :, :, None], chosen, jnp.zeros((), chosen.dtype))
    result = jnp.einsum(
        "pakmn,iakn->pami", regrouped, chosen, preferred_element_type=jnp.float32
    ).astype(jnp.bfloat16)
    return result.reshape(result.shape[0], result.shape[1] * result.shape[2], result.shape[3])


def solution(mesh):
    return jax.shard_map(
        per_device,
        mesh=mesh,
        in_specs=(P(("col", "row"), None, None, None, None), P("col", None), P(), P()),
        out_specs=P("col", "row", None),
        check_vma=False,
    )
```

profile of v0, /device:TPU:1, one launch (start us, length us, event | category | flops | bytes accessed | tf_op | source)
XLA Modules:
  0.0 106.1 jit_solution(12665357266327894407)
XLA Ops:
  6.5 0.0 copy-start
  6.5 0.0 all-gather.3.cloned.1.call-start
  6.5 0.7 all-gather.3.cloned.1.call-update
  7.3 0.0 copy-start.1
  7.3 7.6 %all-to-all-start = ((bf16[1,16,6,128,128]{4,3,2,0,1:T(8,128)(2,1)}), bf16[1,16,6,128,128]{4,3,2,0,1:T(8,128)(2,1)}, u32[]{:S(2)}, u32[]{:S(2)}) async-start(bf16[1,16,6,128,128]{4,3,2,0,1:T(8,128)(2,1)} %bitcast.29), calls=%async_computation | async-start | bytes 6291456 | tf_op jit(solution)/shard_map/all_to_all | solution.py:12
  14.9 0.0 copy-done.1
  14.9 0.6 dynamic-slice
  15.5 0.0 copy-done
  15.5 0.2 dynamic-slice_reduce_fusion
  15.7 0.7 compare_bitcast_fusion
  16.4 70.5 %all-gather.3.cloned.1.call-done = bf16[32,15,2048]{2,1,0:T(8,128)(2,1)} async-done(((bf16[1,15,2048]{2,1,0:T(8,128)(2,1)}), bf16[32,15,2048]{2,1,0:T(8,128)(2,1)}) %all-gather.3.cloned.1.call-update) | async-done | bytes 1966096 | tf_op jit(solution)/shard_map/all_gather | solution.py:18
  86.9 3.4 %reshape.63 = bf16[480,16,128]{2,1,0:T(8,128)(2,1)S(1)} reshape(bf16[32,15,2048]{2,1,0:T(8,128)(2,1)} %all-gather.3.cloned.1.call-done) | data formatting | bytes 3932160 | tf_op jit(solution)/shard_map/reshape | solution.py:20
  90.2 1.8 %copy.6 = bf16[480,16,128]{2,0,1:T(8,128)(2,1)} copy(bf16[480,16,128]{2,1,0:T(8,128)(2,1)S(1)} %reshape.63) | data formatting | bytes 3932160 | tf_op jit(solution)/shard_map/reshape | solution.py:20
  92.0 2.2 %gather_fusion = bf16[6,480,128]{2,1,0:T(8,128)(2,1)S(1)} fusion(bf16[480,16,128]{2,0,1:T(8,128)(2,1)} %copy.6, s32[1024]{0:T(1024)S(1)} %pad_clamp_fusion), kind=kCustom, calls=%fused_computation | custom fusion | bytes 1474584 | tf_op jit(solution)/shard_map/jit(_take)/gather | solution.py:21
  94.3 0.0 all-to-all-done
  94.3 5.0 %fusion.2 = bf16[16,128,480]{1,2,0:T(8,128)(2,1)} fusion(bf16[1,16,6,128,128]{4,3,2,0,1:T(8,128)(2,1)} %all-to-all-done, bf16[6,480,128]{2,1,0:T(8,128)(2,1)S(1)} %gather_fusion, pred[6]{0:T(512)(128)(4,1)S(1)} %compare_bitcast_fusion, pred[6]{0:T(512)(128)(4,1)S(1)} %compare_and_fusion), kind=kOutput, calls=%fused_computation.4 | convolution fusion | flops 1511669760 | bytes 5849100 | tf_op jit(solution)/shard_map/pakmn,iakn->pami/dot_general | solution.py:24
  (3 shorter events, 0.0 us)
Async XLA Ops:
  6.5 9.0 %copy-start = (s32[16,6]{0,1:T(8,128)S(1)}, s32[16,6]{0,1:T(8,128)}, u32[]{:S(2)}) copy-start(s32[16,6]{0,1:T(8,128)} %param.6) | copy-start | bytes 1156
  6.5 80.3 %all-gather.3.cloned.1.call-start = ((), (), s32[]{:S(2)}) async-start(), calls=%async_computation.1 | async-start | bytes 2162688 | tf_op jit(solution)/shard_map/all_gather | solution.py:18
  7.3 7.7 %copy-start.1 = (s32[16]{0:T(128)S(1)}, s32[16]{0:T(128)}, u32[]{:S(2)}) copy-start(s32[16]{0:T(128)} %param.7) | copy-start | bytes 196
  7.3 87.0 %all-to-all-start = ((bf16[1,16,6,128,128]{4,3,2,0,1:T(8,128)(2,1)}), bf16[1,16,6,128,128]{4,3,2,0,1:T(8,128)(2,1)}, u32[]{:S(2)}, u32[]{:S(2)}) async-start(bf16[1,16,6,128,128]{4,3,2,0,1:T(8,128)(2,1)} %bitcast.29), calls=%async_computation | async-start | bytes 6291456 | tf_op jit(solution)/shard_map/all_to_all | solution.py:12
Sparse Core Ops, SparseCore 0:
  9.5 77.3 all-gather.2
where the time goes:
time: 106 us
  waiting for transfers between devices  71.2 us (67%)
  between operations  13.5 us (13%)
  local copies, waits for them, and re-layouts  8.14 us (8%)
  starting transfers between devices  7.64 us (7%)
  matrix products  4.96 us (5%)
    all_gather x1, waiting for transfers between devices, per_device(): whole_green = lax.all_gather(green_panel, 'col', axis=0, tiled=True)  70.5 us
    all_to_all x1, starting transfers between devices, per_device(): lax.all_to_all(integrals, 'row', split_axis=1, concat_axis=0, tiled=True)  7.64 us
    reshape x2, local copies, waits for them, and re-layouts, per_device(): spread = whole_green.reshape(panel_rows, atom_count, block_width)  5.13 us
    dot_general x1, matrix products, per_device(): jnp.einsum('pakmn,iakn->pami', regrouped, chosen, preferred_element_type=...  4.96 us
    gather x1, local copies, waits for them, and re-layouts, per_device(): chosen = jnp.take(spread, links_part.reshape(-1), axis=1)  2.23 us
  transfers between devices with their start and end apart: 2, of which 1 were waited for; matrix products, arithmetic and copies ran while one was open for 8% of the time, Pallas kernels for 0%

commit v1 on v0

v1 whole, which is shorter than its diff:
```python
import jax
import jax.numpy as jnp
from jax import lax
from jax.sharding import PartitionSpec as P


def per_device(integrals, green_panel, neighbours, slot_counts):
    atom_count = neighbours.shape[0]
    slot_count = neighbours.shape[1]
    block_width = integrals.shape[-1]
    keep = jnp.arange(slot_count, dtype=jnp.int32)[None, :] < slot_counts[:, None]
    green = lax.all_gather(green_panel, "col", axis=0, tiled=True)
    rows = green.shape[0]
    spread = green.reshape(rows, atom_count, block_width)
    chosen = jnp.take(spread, neighbours.reshape(-1), axis=1)
    chosen = chosen.reshape(rows, atom_count, slot_count, block_width)
    chosen = jnp.where(keep[None, :, :, None], chosen, jnp.zeros((), chosen.dtype))
    local = integrals[0]
    out = jnp.einsum(
        "akmn,iakn->ami", local, chosen, preferred_element_type=jnp.float32
    ).astype(jnp.bfloat16)
    out = lax.all_to_all(out, "row", split_axis=0, concat_axis=0, tiled=True)
    return out


def solution(mesh):
    return jax.shard_map(
        per_device,
        mesh=mesh,
        in_specs=(P(("col", "row"), None, None, None, None), P("col", None), P(), P()),
        out_specs=P("col", "row", None),
        check_vma=False,
    )
```

time: 106 us -> 151 us (1.42)
  blocking collectives: 0 us -> 32.3 us
  local copies, waits for them, and re-layouts: 8.14 us -> 18.5 us
  starting transfers between devices: 7.64 us -> 0.01 us
  waiting for transfers between devices: 71.2 us -> 77.9 us
  matrix products: 4.96 us -> 7.61 us
    all_to_all x0 -> x1, blocking collectives: none -> 32.3 us  [per_device(): out = lax.all_to_all(out, 'row', split_axis=0, concat_axis=0, tiled=True)]
    all_to_all x1 -> x0, starting transfers between devices: 7.64 us -> none  [per_device(): lax.all_to_all(integrals, 'row', split_axis=1, concat_axis=0, tiled=True)]
    all_gather x1, waiting for transfers between devices: 70.5 us -> 77.2 us  [per_device(): green = lax.all_gather(green_panel, 'col', axis=0, tiled=True)]
    gather x1, local copies, waits for them, and re-layouts: 2.23 us -> 8.25 us  [per_device(): chosen = jnp.take(spread, neighbours.reshape(-1), axis=1)]
    reshape x2 -> x3, local copies, waits for them, and re-layouts: 5.13 us -> 7.85 us  [the longest x2 7.76 us: per_device(): spread = green.reshape(rows, atom_count, block_width)]
    dot_general x1, matrix products: 4.96 us -> 7.61 us  [per_device(): jnp.einsum('akmn,iakn->ami', local, chosen, preferred_element_type=jnp.fl...]
    unnamed x4, local copies, waits for them, and re-layouts: 0.01 us -> 2.26 us
  transfers between devices with their start and end apart: 2 -> 1, of which waited for: 1 -> 1; matrix products, arithmetic and copies ran while one was open for 8% -> 2% of each run, Pallas kernels for 0% -> 0%
where the time goes in v1:
time: 151 us
  waiting for transfers between devices  77.9 us (52%)
  blocking collectives  32.3 us (21%)
  local copies, waits for them, and re-layouts  18.5 us (12%)
  between operations  13.4 us (9%)
  matrix products  7.61 us (5%)
    all_gather x1, waiting for transfers between devices, per_device(): green = lax.all_gather(green_panel, 'col', axis=0, tiled=True)  77.2 us
    all_to_all x1, blocking collectives, per_device(): out = lax.all_to_all(out, 'row', split_axis=0, concat_axis=0, tiled=True)  32.3 us
    gather x1, local copies, waits for them, and re-layouts, per_device(): chosen = jnp.take(spread, neighbours.reshape(-1), axis=1)  8.25 us
    reshape x2, local copies, waits for them, and re-layouts, per_device(): spread = green.reshape(rows, atom_count, block_width)  7.76 us
    dot_general x1, matrix products, per_device(): jnp.einsum('akmn,iakn->ami', local, chosen, preferred_element_type=jnp.fl...  7.61 us
  transfers between devices with their start and end apart: 1, of which 1 were waited for; matrix products, arithmetic and copies ran while one was open for 2% of the time, Pallas kernels for 0%

profile of v1, /device:TPU:1, one launch (start us, length us, event | category | flops | bytes accessed | tf_op | source)
XLA Modules:
  0.0 151.1 jit_solution(5869147171408039728)
XLA Ops:
  6.5 0.0 copy-start
  6.5 0.0 all-gather.3.cloned.1.call-start
  6.5 0.7 all-gather.3.cloned.1.call-update
  7.3 1.0 copy.12
  8.2 0.1 reshape.65
  8.3 0.7 compare_and_fusion
  9.0 0.1 copy.11
  9.1 0.7 iota_compare_fusion
  9.9 77.2 %all-gather.3.cloned.1.call-done = bf16[32,15,2048]{2,1,0:T(8,128)(2,1)} async-done(((bf16[1,15,2048]{2,1,0:T(8,128)(2,1)}), bf16[32,15,2048]{2,1,0:T(8,128)(2,1)}) %all-gather.3.cloned.1.call-update) | async-done | bytes 1966096 | tf_op jit(solution)/shard_map/all_gather | solution.py:12
  87.0 4.3 %reshape.64 = bf16[480,16,128]{2,1,0:T(8,128)(2,1)} reshape(bf16[32,15,2048]{2,1,0:T(8,128)(2,1)} %all-gather.3.cloned.1.call-done) | data formatting | bytes 3932160 | tf_op jit(solution)/shard_map/reshape | solution.py:14
  91.3 3.4 %copy.13 = bf16[480,16,128]{2,0,1:T(8,128)(2,1)} copy(bf16[480,16,128]{2,1,0:T(8,128)(2,1)} %reshape.64) | data formatting | bytes 3932160 | tf_op jit(solution)/shard_map/reshape | solution.py:14
  94.8 8.3 %gather_fusion = bf16[96,480,128]{2,1,0:T(8,128)(2,1)} fusion(bf16[480,16,128]{2,0,1:T(8,128)(2,1)} %copy.13, s32[1024]{0:T(1024)S(1)} %pad_clamp_fusion), kind=kCustom, calls=%fused_computation | custom fusion | bytes 23593344 | tf_op jit(solution)/shard_map/jit(_take)/gather | solution.py:15
  103.0 0.0 copy-done
  103.0 7.6 %fusion.8 = bf16[16,128,480]{1,2,0:T(8,128)(2,1)S(1)} fusion(bf16[1,16,6,128,128]{4,3,2,1,0:T(8,128)(2,1)S(1)} %copy-done, bf16[480,16,6,128]{3,0,2,1:T(8,128)(2,1)} %bitcast.18, pred[16,6]{1,0:T(8,128)(4,1)S(1)} %copy.11, pred[16,6]{1,0:T(8,128)(4,1)S(1)} %iota_compare_fusion), kind=kOutput, calls=%fused_computation.10 | convolution fusion | flops 1522728960 | bytes 16908480 | tf_op jit(solution)/shard_map/akmn,iakn->ami/dot_general | solution.py:19
  110.7 32.3 %all_to_all.5 = bf16[16,128,480]{1,2,0:T(8,128)(2,1)S(1)} all-to-all(bf16[16,128,480]{1,2,0:T(8,128)(2,1)S(1)} %fusion.8), channel_id=1, replica_groups=mesh['row'=16,'col'=32] {'row'}, dimensions={0} | all-to-all | bytes 3932160 | tf_op jit(solution)/shard_map/all_to_all | solution.py:22
  143.0 1.3 copy.16
  (2 shorter events, 0.0 us)
Async XLA Ops:
  6.5 96.5 %copy-start = (bf16[1,16,6,128,128]{4,3,2,1,0:T(8,128)(2,1)S(1)}, bf16[1,16,6,128,128]{4,3,2,1,0:T(8,128)(2,1)}, u32[]{:S(2)}) copy-start(bf16[1,16,6,128,128]{4,3,2,1,0:T(8,128)(2,1)} %param.4) | copy-start | bytes 9437188
  6.5 80.5 %all-gather.3.cloned.1.call-start = ((), (), s32[]{:S(2)}) async-start(), calls=%async_computation.1 | async-start | bytes 2162688 | tf_op jit(solution)/shard_map/all_gather | solution.py:12
Sparse Core Ops, SparseCore 0:
  9.5 77.5 all-gather.2

commit v2 on v1

v2 whole, which is shorter than its diff:
```python
import functools

import jax
import jax.numpy as jnp
from jax import lax
from jax.experimental import pallas as pl
from jax.experimental.pallas import tpu as pltpu
from jax.sharding import PartitionSpec as P

MESH = pl.DeviceIdType.MESH
SIDE = 4
DEPTH = 16
FAR = DEPTH // 2
ATOMS = 16
SLOTS = 6
BS = 128
PANEL = 15
SHARD = 16
NOCC = 480
WIDE = SLOTS * BS
PARTS = 2
CHUNKS = 2
HALF = BS // 2
ROWS = HALF // CHUNKS
NU = ATOMS // PARTS


def kernel(
    ints, panel, nbr, cnt, out,
    g0, g1, g2, g3, g4, g5, g6, g7, g8,
    rows, mid, fin, w32, obuf,
    ring_s, ring_r, sib_s, sib_r, one_s, one_r, two_s, two_r, local, osem,
):
    green = [g0, g1, g2, g3, g4, g5, g6, g7, g8]
    row = lax.axis_index("row")
    col = lax.axis_index("col")
    x, y = row // SIDE, row % SIDE
    z, core = col // 2, col % 2

    def at(dx=0, dy=0, dz=0, dc=0):
        return (
            ((x + dx) % SIDE) * SIDE + (y + dy) % SIDE,
            ((z + dz + DEPTH) % DEPTH) * 2 + (core + dc) % 2,
        )

    partners = [at(dx=d) for d in (1, 2, 3)] + [at(dy=d) for d in (1, 2, 3)]
    partners += [at(dz=1), at(dz=-1), at(dc=1)]
    barrier = pltpu.get_barrier_semaphore()
    for p in partners:
        pl.semaphore_signal(barrier, inc=1, device_id=p, device_id_type=MESH)

    load = pltpu.make_async_copy(panel, rows, local.at[0])
    load.start()
    span = [pl.ds(h * HALF + c * ROWS, ROWS) for h in range(2) for c in range(CHUNKS)]

    def source(h, c, d):
        m = span[h * CHUNKS + c]
        if h == 0:
            return ints.at[(x + d) % SIDE, :, :, m, :]
        return ints.at[:, (y + d) % SIDE, :, m, :]

    own = []
    for h in range(2):
        for c in range(CHUNKS):
            cp = pltpu.make_async_copy(
                source(h, c, 0), mid.at[h, c, 0], local.at[1 + h * CHUNKS + c]
            )
            cp.start()
            own.append(cp)
    load.wait()
    for nu in range(ATOMS):
        g0[nu, pl.ds(0, SHARD), :] = jnp.concatenate(
            [rows[:, nu * BS : (nu + 1) * BS], jnp.zeros((1, BS), jnp.bfloat16)], axis=0
        )
    w32[...] = jnp.zeros_like(w32)
    pl.semaphore_wait(barrier, len(partners))

    def nus(p):
        return pl.ds(p * NU, NU)

    def ring(d, q, p):
        q_src = 0 if d == 0 else q
        q_dst = 0 if d + 1 == FAR else q
        return pltpu.make_async_remote_copy(
            src_ref=green[d].at[nus(p), pl.ds(q_src * SHARD, SHARD), :],
            dst_ref=green[d + 1].at[nus(p), pl.ds(q_dst * SHARD, SHARD), :],
            send_sem=ring_s.at[d, q, p],
            recv_sem=ring_r.at[d, q, p],
            device_id=at(dz=1 if q == 0 else -1),
            device_id_type=MESH,
        )

    def moves(d, q, p):
        return d + 1 < FAR or q == p

    def shared(d):
        return 1 if d in (0, FAR) else 2

    def sib(d, q):
        n = shared(d)
        return pltpu.make_async_remote_copy(
            src_ref=green[d].at[:, pl.ds(q * SHARD, SHARD), :],
            dst_ref=green[d].at[:, pl.ds((q + n) * SHARD, SHARD), :],
            send_sem=sib_s.at[d, q],
            recv_sem=sib_r.at[d, q],
            device_id=at(dc=1),
            device_id_type=MESH,
        )

    def first(h, c, d):
        return pltpu.make_async_remote_copy(
            src_ref=source(h, c, d),
            dst_ref=mid.at[h, c, d],
            send_sem=one_s.at[h, c, d],
            recv_sem=one_r.at[h, c, d],
            device_id=at(dx=d) if h == 0 else at(dy=d),
            device_id_type=MESH,
        )

    def held(h, c, e):
        return mid.at[h, c, :, (y + e) % SIDE if h == 0 else (x + e) % SIDE]

    def second(h, c, e):
        return pltpu.make_async_remote_copy(
            src_ref=held(h, c, e),
            dst_ref=fin.at[h, c, e],
            send_sem=two_s.at[h, c, e],
            recv_sem=two_r.at[h, c, e],
            device_id=at(dy=e) if h == 0 else at(dx=e),
            device_id_type=MESH,
        )

    def keep(h, c):
        return pltpu.make_async_copy(
            held(h, c, 0), fin.at[h, c, 0], local.at[1 + (2 + h) * CHUNKS + c]
        )

    def ring_step(d):
        for p in range(PARTS):
            for q in range(2):
                if moves(d - 1, q, p):
                    ring(d - 1, q, p).wait_recv()
                    if d < FAR and moves(d, q, p):
                        ring(d, q, p).start()
        for q in range(shared(d)):
            sib(d, q).start()

    def forward(c):
        for h in range(2):
            own[h * CHUNKS + c].wait()
            for d in (1, 3, 2):
                first(h, c, d).wait_recv()
            for e in (1, 3, 2):
                second(h, c, e).start()
            keep(h, c).start()

    def weigh(d):
        n = shared(d)
        for q in range(n):
            sib(d, q).wait_recv()
        lanes = 2 * n * SHARD
        at_row = lax.broadcasted_iota(jnp.int32, (NOCC, lanes), 0)
        lane = lax.broadcasted_iota(jnp.int32, (NOCC, lanes), 1)
        q, j = lane // SHARD, lane % SHARD
        if n == 2:
            from_z = jnp.where(q % 2 == 0, z - d + DEPTH, z + d) % DEPTH
        else:
            from_z = (z + d) % DEPTH
        from_core = jnp.where(q < n, core, 1 - core)
        to = (from_z * 2 + from_core) * PANEL + j
        place = ((to == at_row) & (j < PANEL)).astype(jnp.float32).astype(jnp.bfloat16)
        parts = []
        for k in range(SLOTS):
            g = green[d][nbr[row, k], pl.ds(0, lanes), :]
            parts.append(jnp.where(k < cnt[row], g, jnp.zeros_like(g)))
        w32[...] += jnp.dot(
            place, jnp.concatenate(parts, axis=1), preferred_element_type=jnp.float32
        )

    def contract(c):
        for h in range(2):
            keep(h, c).wait()
            for e in (1, 3, 2):
                second(h, c, e).wait_recv()
            blocks = [
                fin[h, c, :, :, k].reshape(SIDE * SIDE * ROWS, BS) for k in range(SLOTS)
            ]
            lhs = jnp.concatenate(blocks, axis=1)
            res = lax.dot_general(
                lhs, w32[...].astype(jnp.bfloat16), (((1,), (1,)), ((), ())),
                preferred_element_type=jnp.float32,
            ).astype(jnp.bfloat16)
            res = res.reshape(SIDE, SIDE, ROWS, NOCC)
            for e in range(SIDE):
                for d in range(SIDE):
                    dx, dy = (d, e) if h == 0 else (e, d)
                    p = ((x - dx + SIDE) % SIDE) * SIDE + (y - dy + SIDE) % SIDE
                    obuf[p, span[h * CHUNKS + c], :] = res[e, d]

    for p in range(PARTS):
        for q in range(2):
            ring(0, q, p).start()
    sib(0, 0).start()
    for c in range(CHUNKS):
        for d in (1, 3, 2):
            for h in range(2):
                first(h, c, d).start()

    ring_step(1)
    weigh(0)
    ring_step(2)
    weigh(1)
    ring_step(3)
    weigh(2)
    forward(0)
    ring_step(4)
    weigh(3)
    ring_step(5)
    weigh(4)
    forward(1)
    ring_step(6)
    weigh(5)
    ring_step(7)
    weigh(6)
    ring_step(8)
    weigh(7)
    weigh(8)
    contract(0)
    contract(1)
    store = pltpu.make_async_copy(obuf, out, osem)
    store.start()

    for d in range(FAR):
        for q in range(2):
            for p in range(PARTS):
                if moves(d, q, p):
                    ring(d, q, p).wait_send()
    for d in range(FAR + 1):
        for q in range(shared(d)):
            sib(d, q).wait_send()
    for h in range(2):
        for c in range(CHUNKS):
            for d in (1, 3, 2):
                first(h, c, d).wait_send()
                second(h, c, d).wait_send()
    store.wait()


def per_device(integrals, green_panel, neighbours, slot_counts):
    blocks = integrals.reshape(SIDE, SIDE, SLOTS, BS, BS)
    hbm = pl.BlockSpec(memory_space=pl.ANY)
    smem = pl.BlockSpec(memory_space=pltpu.SMEM)
    bf16, f32 = jnp.bfloat16, jnp.float32
    dma = pltpu.SemaphoreType.DMA
    return pl.pallas_call(
        kernel,
        out_shape=jax.ShapeDtypeStruct((ATOMS, BS, NOCC), bf16),
        in_specs=[hbm, hbm, smem, smem],
        out_specs=hbm,
        scratch_shapes=[pltpu.VMEM((ATOMS, 4 * SHARD, BS), bf16)] * (FAR + 1)
        + [
            pltpu.VMEM((PANEL, ATOMS * BS), bf16),
            pltpu.VMEM((2, CHUNKS, SIDE, SIDE, SLOTS, ROWS, BS), bf16),
            pltpu.VMEM((2, CHUNKS, SIDE, SIDE, SLOTS, ROWS, BS), bf16),
            pltpu.VMEM((NOCC, WIDE), f32),
            pltpu.VMEM((ATOMS, BS, NOCC), bf16),
            dma((FAR, 2, PARTS)),
            dma((FAR, 2, PARTS)),
            dma((FAR + 1, 2)),
            dma((FAR + 1, 2)),
            dma((2, CHUNKS, SIDE)),
            dma((2, CHUNKS, SIDE)),
            dma((2, CHUNKS, SIDE)),
            dma((2, CHUNKS, SIDE)),
            dma((1 + 4 * CHUNKS,)),
            dma,
        ],
        compiler_params=pltpu.CompilerParams(
            collective_id=0, has_side_effects=True, vmem_limit_bytes=56 << 20
        ),
    )(blocks, green_panel, neighbours, slot_counts)


def solution(mesh):
    return jax.shard_map(
        per_device,
        mesh=mesh,
        in_specs=(P(("col", "row"), None, None, None, None), P("col", None), P(), P()),
        out_specs=P("col", "row", None),
        check_vma=False,
    )
```

time: 151 us -> 58.4 us (0.39)
  waiting for transfers between devices: 77.9 us -> 0 us
  Pallas kernels: 0 us -> 52.8 us
  blocking collectives: 32.3 us -> 0 us
  between operations: 13.4 us -> 0.01 us
  local copies, waits for them, and re-layouts: 18.5 us -> 5.26 us
  matrix products: 7.61 us -> 0 us
    all_gather x1 -> x0, waiting for transfers between devices: 77.2 us -> none  [per_device(): green = lax.all_gather(green_panel, 'col', axis=0, tiled=True)]
    pallas_call x0 -> x1, Pallas kernels: none -> 52.8 us  [per_device(): pl.pallas_call(kernel, out_shape=jax.ShapeDtypeStruct((ATOMS, BS, NOCC),...]
    all_to_all x1 -> x0, blocking collectives: 32.3 us -> none  [per_device(): out = lax.all_to_all(out, 'row', split_axis=0, concat_axis=0, tiled=True)]
    gather x1 -> x0, local copies, waits for them, and re-layouts: 8.25 us -> none  [per_device(): chosen = jnp.take(spread, neighbours.reshape(-1), axis=1)]
    reshape x3 -> x0, local copies, waits for them, and re-layouts: 7.85 us -> none  [the longest x2 7.76 us: per_device(): spread = green.reshape(rows, atom_count, block_width)]
    dot_general x1 -> x0, matrix products: 7.61 us -> none  [per_device(): jnp.einsum('akmn,iakn->ami', local, chosen, preferred_element_type=jnp.fl...]
    pallas_call x0 -> x1, local copies, waits for them, and re-layouts: none -> 3.9 us  [per_device(): pl.pallas_call(kernel, out_shape=jax.ShapeDtypeStruct((ATOMS, BS, NOCC),...]
  transfers between devices with their start and end apart: 1 -> 0, of which waited for: 1 -> 0; matrix products, arithmetic and copies ran while one was open for 2% -> 0% of each run, Pallas kernels for 0% -> 0%
where the time goes in v2:
time: 58.4 us; the launch traced here: 58.1 us
  Pallas kernels  52.8 us (90%)
  local copies, waits for them, and re-layouts  5.26 us (9%)
    pallas_call x1, Pallas kernels, per_device(): pl.pallas_call(kernel, out_shape=jax.ShapeDtypeStruct((ATOMS, BS, NOCC),...  52.8 us
    pallas_call x1, local copies, waits for them, and re-layouts, per_device(): pl.pallas_call(kernel, out_shape=jax.ShapeDtypeStruct((ATOMS, BS, NOCC),...  3.9 us
    unnamed x1, local copies, waits for them, and re-layouts  1.36 us

profile of v2, /device:TPU:1, one launch (start us, length us, event | category | flops | bytes accessed | tf_op | source)
XLA Modules:
  0.0 58.1 jit_solution(17720868577258860851)
XLA Ops:
  0.0 1.4 %copy.5.nbr = s32[16,6]{1,0:T(8,128)} copy(s32[16,6]{0,1:T(8,128)} %param.6) | data formatting | bytes 768 | tf_op args[2]
  1.4 52.8 %shard_map.46 = bf16[16,128,480]{2,1,0:T(8,128)(2,1)} custom-call(bf16[4,4,6,128,128]{4,3,2,1,0:T(8,128)(2,1)} %bitcast.1, bf16[15,2048]{1,0:T(8,128)(2,1)} %panel.1, s32[16,6]{1,0:T(8,128)} %copy.5.nbr, s32[16]{0:T(128)} %cnt.1), custom_call_target="tpu_custom_call" | custom-call | tf_op jit(solution)/shard_map/pallas_call | solution.py:255
  54.2 3.9 %copy.6 = bf16[16,128,480]{1,2,0:T(8,128)(2,1)} copy(bf16[16,128,480]{2,1,0:T(8,128)(2,1)} %shard_map.46) | data formatting | bytes 3932160 | tf_op jit(solution)/shard_map/pallas_call | solution.py:255

commit v3 on v2

v3 whole, which is shorter than its diff:
```python
import functools

import jax
import jax.numpy as jnp
from jax import lax
from jax.experimental import pallas as pl
from jax.experimental.pallas import tpu as pltpu
from jax.sharding import PartitionSpec as P

MESH = pl.DeviceIdType.MESH
SIDE = 4
DEPTH = 16
FAR = DEPTH // 2
ATOMS = 16
SLOTS = 6
BS = 128
PANEL = 15
SHARD = 16
NOCC = 480
WIDE = SLOTS * BS
PARTS = 2
HALF = SLOTS // 2
CHUNKS = HALF
NU = ATOMS // PARTS
GROUP = 4


def exchange(
    ints, panel, nbr_in, cnt_in, fin, wout,
    g0, g1, g2, g3, g4, g5, g6, g7, g8,
    nbr, cnt, rows, mid, w32, w16,
    ready, ring_s, ring_r, sib_s, sib_r, one_s, one_r, two_s, two_r, local,
):
    green = [g0, g1, g2, g3, g4, g5, g6, g7, g8]
    row = lax.axis_index("row")
    col = lax.axis_index("col")
    x, y = row // SIDE, row % SIDE
    z, core = col // 2, col % 2

    def at(dx=0, dy=0, dz=0, dc=0):
        return (
            ((x + dx) % SIDE) * SIDE + (y + dy) % SIDE,
            ((z + dz + DEPTH) % DEPTH) * 2 + (core + dc) % 2,
        )

    up_first = z >= FAR + 1
    down_first = (z >= 1) & (z <= FAR + 1)
    partners = [at(dx=d) for d in (1, 2, 3)] + [at(dy=d) for d in (1, 2, 3)] + [at(dc=1)]
    barrier = pltpu.get_barrier_semaphore()
    for p in partners:
        pl.semaphore_signal(barrier, inc=1, device_id=p, device_id_type=MESH)

    @pl.when(jnp.logical_not(up_first))
    def _():
        pl.semaphore_signal(barrier, inc=1, device_id=at(dz=1), device_id_type=MESH)

    @pl.when(jnp.logical_not(down_first))
    def _():
        pl.semaphore_signal(barrier, inc=1, device_id=at(dz=-1), device_id_type=MESH)

    load = pltpu.make_async_copy(panel, rows, local.at[0])
    load.start()
    tables = [
        pltpu.make_async_copy(nbr_in, nbr, local.at[1 + 4 * CHUNKS]),
        pltpu.make_async_copy(cnt_in, cnt, local.at[2 + 4 * CHUNKS]),
    ]
    for cp in tables:
        cp.start()

    def source(h, c, d):
        if h == 0:
            return ints.at[(x + d) % SIDE, :, c]
        return ints.at[:, (y + d) % SIDE, HALF + c]

    def landing(h, c):
        return mid.at[h, c, x if h == 0 else y]

    own = []
    for c in range(CHUNKS):
        for h in range(2):
            cp = pltpu.make_async_copy(
                source(h, c, 0), landing(h, c), local.at[1 + h * CHUNKS + c]
            )
            cp.start()
            own.append(cp)
    load.wait()
    for nu in range(ATOMS):
        g0[nu, pl.ds(0, SHARD), :] = jnp.concatenate(
            [rows[:, nu * BS : (nu + 1) * BS], jnp.zeros((1, BS), jnp.bfloat16)], axis=0
        )
    w32[...] = jnp.zeros_like(w32)
    expected = len(partners) + up_first.astype(jnp.int32) + down_first.astype(jnp.int32)
    pl.semaphore_wait(barrier, expected)

    @pl.when(up_first)
    def _():
        pl.semaphore_signal(ready.at[0], inc=1, device_id=at(dz=1), device_id_type=MESH)

    @pl.when(down_first)
    def _():
        pl.semaphore_signal(ready.at[1], inc=1, device_id=at(dz=-1), device_id_type=MESH)

    def nus(p):
        return pl.ds(p * NU, NU)

    def ring(d, q, p):
        q_src = 0 if d == 0 else q
        q_dst = 0 if d + 1 == FAR else q
        return pltpu.make_async_remote_copy(
            src_ref=green[d].at[nus(p), pl.ds(q_src * SHARD, SHARD), :],
            dst_ref=green[d + 1].at[nus(p), pl.ds(q_dst * SHARD, SHARD), :],
            send_sem=ring_s.at[d, q, p],
            recv_sem=ring_r.at[d, q, p],
            device_id=at(dz=1 if q == 0 else -1),
            device_id_type=MESH,
        )

    def moves(d, q, p):
        return d + 1 < FAR or q == p

    def shared(d):
        return 1 if d in (0, FAR) else 2

    def sib(d, q):
        n = shared(d)
        return pltpu.make_async_remote_copy(
            src_ref=green[d].at[:, pl.ds(q * SHARD, SHARD), :],
            dst_ref=green[d].at[:, pl.ds((q + n) * SHARD, SHARD), :],
            send_sem=sib_s.at[d, q],
            recv_sem=sib_r.at[d, q],
            device_id=at(dc=1),
            device_id_type=MESH,
        )

    def first(h, c, d):
        return pltpu.make_async_remote_copy(
            src_ref=source(h, c, d),
            dst_ref=landing(h, c),
            send_sem=one_s.at[h, c, d],
            recv_sem=one_r.at[h, c, d],
            device_id=at(dx=d) if h == 0 else at(dy=d),
            device_id_type=MESH,
        )

    def held(h, c, e):
        return mid.at[h, c, :, (y + e) % SIDE if h == 0 else (x + e) % SIDE]

    def final(h, c):
        return fin.at[:, y, c] if h == 0 else fin.at[x, :, HALF + c]

    def second(h, c, e):
        return pltpu.make_async_remote_copy(
            src_ref=held(h, c, e),
            dst_ref=final(h, c),
            send_sem=two_s.at[h, c, e],
            recv_sem=two_r.at[h, c, e],
            device_id=at(dy=e) if h == 0 else at(dx=e),
            device_id_type=MESH,
        )

    def keep(h, c):
        return pltpu.make_async_copy(
            held(h, c, 0), final(h, c), local.at[1 + (2 + h) * CHUNKS + c]
        )

    def ring_step(d):
        for p in range(PARTS):
            for q in range(2):
                if moves(d - 1, q, p):
                    ring(d - 1, q, p).wait_recv()
                    if d < FAR and moves(d, q, p):
                        ring(d, q, p).start()
        for q in range(shared(d)):
            sib(d, q).start()

    def forward(c):
        for h in range(2):
            own[c * 2 + h].wait()
            for d in (1, 3, 2):
                first(h, c, d).wait_recv()
            for e in (1, 3, 2):
                second(h, c, e).start()
            keep(h, c).start()

    def weigh(d):
        n = shared(d)
        for q in range(n):
            sib(d, q).wait_recv()
        lanes = 2 * n * SHARD
        at_row = lax.broadcasted_iota(jnp.int32, (NOCC, lanes), 0)
        lane = lax.broadcasted_iota(jnp.int32, (NOCC, lanes), 1)
        q, j = lane // SHARD, lane % SHARD
        if n == 2:
            from_z = jnp.where(q % 2 == 0, z - d + DEPTH, z + d) % DEPTH
        else:
            from_z = (z + d) % DEPTH
        from_core = jnp.where(q < n, core, 1 - core)
        to = (from_z * 2 + from_core) * PANEL + j
        place = ((to == at_row) & (j < PANEL)).astype(jnp.float32).astype(jnp.bfloat16)
        parts = []
        for k in range(SLOTS):
            g = green[d][nbr[k, row], pl.ds(0, lanes), :]
            parts.append(jnp.where(k < cnt[row], g, jnp.zeros_like(g)))
        w32[...] += jnp.dot(
            place, jnp.concatenate(parts, axis=1), preferred_element_type=jnp.float32
        )

    def depart(q):
        for p in range(PARTS):
            ring(0, q, p).start()

    for c in range(CHUNKS):
        for d in (1, 3, 2):
            for h in range(2):
                first(h, c, d).start()
    sib(0, 0).start()

    @pl.when(up_first)
    def _():
        depart(0)

    @pl.when(down_first)
    def _():
        depart(1)

    @pl.when(jnp.logical_not(up_first))
    def _():
        pl.semaphore_wait(ready.at[1], 1)
        depart(0)

    @pl.when(jnp.logical_not(down_first))
    def _():
        pl.semaphore_wait(ready.at[0], 1)
        depart(1)

    for cp in tables:
        cp.wait()
    for d in range(1, FAR + 1):
        ring_step(d)
        if 3 <= d < 3 + CHUNKS:
            forward(d - 3)
        weigh(d - 1)
    weigh(FAR)
    w16[...] = w32[...].astype(jnp.bfloat16)
    store = pltpu.make_async_copy(w16, wout, local.at[0])
    store.start()

    for h in range(2):
        for c in range(CHUNKS):
            keep(h, c).wait()
            for d in (1, 3, 2):
                first(h, c, d).wait_send()
                second(h, c, d).wait_send()
                second(h, c, d).wait_recv()
    for d in range(FAR):
        for q in range(2):
            for p in range(PARTS):
                if moves(d, q, p):
                    ring(d, q, p).wait_send()
    for d in range(FAR + 1):
        for q in range(shared(d)):
            sib(d, q).wait_send()
    store.wait()


def contract(blocks, weights, out):
    flat = [blocks[:, k].reshape(GROUP * BS, BS) for k in range(SLOTS)]
    res = lax.dot_general(
        weights[...], jnp.concatenate(flat, axis=1), (((1,), (1,)), ((), ())),
        preferred_element_type=jnp.float32,
    )
    for p in range(GROUP):
        out[p] = res[:, p * BS : (p + 1) * BS].astype(jnp.bfloat16)


def per_device(integrals, green_panel, neighbours, slot_counts):
    blocks = integrals.reshape(SIDE, SIDE, SLOTS, BS, BS)
    anywhere = pl.BlockSpec(memory_space=pl.ANY)
    bf16, f32 = jnp.bfloat16, jnp.float32
    dma = pltpu.SemaphoreType.DMA
    gathered, weights = pl.pallas_call(
        exchange,
        out_shape=[
            jax.ShapeDtypeStruct((SIDE, SIDE, SLOTS, BS, BS), bf16),
            jax.ShapeDtypeStruct((NOCC, WIDE), bf16),
        ],
        in_specs=[pl.BlockSpec(memory_space=pltpu.HBM)] * 4,
        out_specs=[anywhere, anywhere],
        scratch_shapes=[pltpu.VMEM((ATOMS, 4 * SHARD, BS), bf16)] * (FAR + 1)
        + [
            pltpu.SMEM((SLOTS, ATOMS), jnp.int32),
            pltpu.SMEM((ATOMS,), jnp.int32),
            pltpu.VMEM((PANEL, ATOMS * BS), bf16),
            pltpu.VMEM((2, CHUNKS, SIDE, SIDE, BS, BS), bf16),
            pltpu.VMEM((NOCC, WIDE), f32),
            pltpu.VMEM((NOCC, WIDE), bf16),
            pltpu.SemaphoreType.REGULAR((2,)),
            dma((FAR, 2, PARTS)),
            dma((FAR, 2, PARTS)),
            dma((FAR + 1, 2)),
            dma((FAR + 1, 2)),
            dma((2, CHUNKS, SIDE)),
            dma((2, CHUNKS, SIDE)),
            dma((2, CHUNKS, SIDE)),
            dma((2, CHUNKS, SIDE)),
            dma((3 + 4 * CHUNKS,)),
        ],
        compiler_params=pltpu.CompilerParams(
            collective_id=0, has_side_effects=True, vmem_limit_bytes=48 << 20
        ),
    )(blocks, green_panel, neighbours.T, slot_counts)
    result = pl.pallas_call(
        contract,
        grid=(ATOMS // GROUP,),
        out_shape=jax.ShapeDtypeStruct((ATOMS, NOCC, BS), bf16),
        in_specs=[
            pl.BlockSpec((GROUP, SLOTS, BS, BS), lambda g: (g, 0, 0, 0)),
            pl.BlockSpec((NOCC, WIDE), lambda g: (0, 0)),
        ],
        out_specs=pl.BlockSpec((GROUP, NOCC, BS), lambda g: (g, 0, 0)),
        compiler_params=pltpu.CompilerParams(vmem_limit_bytes=48 << 20),
    )(gathered.reshape(ATOMS, SLOTS, BS, BS), weights)
    return jnp.swapaxes(result, 1, 2)


def solution(mesh):
    return jax.shard_map(
        per_device,
        mesh=mesh,
        in_specs=(P(("col", "row"), None, None, None, None), P("col", None), P(), P()),
        out_specs=P("col", "row", None),
        check_vma=False,
    )
```

time: 58.4 us -> 51.1 us (0.88)
  Pallas kernels: 52.8 us -> 48.7 us
  local copies, waits for them, and re-layouts: 5.26 us -> 2.18 us
    pallas_call x1 -> x2, Pallas kernels: 52.8 us -> 48.7 us  [the longest x1 45.4 us: per_device(): pl.pallas_call(exchange, out_shape=[jax.ShapeDtypeStruct((SIDE, SIDE, SLO...]
    pallas_call x1 -> x0, local copies, waits for them, and re-layouts: 3.9 us -> none  [per_device(): pl.pallas_call(kernel, out_shape=jax.ShapeDtypeStruct((ATOMS, BS, NOCC),...]
    unnamed x1 -> x6, local copies, waits for them, and re-layouts: 1.36 us -> 2.18 us
where the time goes in v3:
time: 51.1 us; the launch traced here: 50.9 us
  Pallas kernels  48.7 us (95%)
  local copies, waits for them, and re-layouts  2.18 us (4%)
    pallas_call x1, Pallas kernels, per_device(): pl.pallas_call(exchange, out_shape=[jax.ShapeDtypeStruct((SIDE, SIDE, SLO...  45.4 us
    pallas_call x1, Pallas kernels, per_device(): pl.pallas_call(contract, grid=(ATOMS // GROUP,), out_shape=jax.ShapeDtype...  3.34 us
    unnamed x6, local copies, waits for them, and re-layouts  2.18 us

profile of v3, /device:TPU:1, one launch (start us, length us, event | category | flops | bytes accessed | tf_op | source)
XLA Modules:
  0.0 50.9 jit_solution(1576543584782610505)
XLA Ops:
  0.0 0.0 copy-start
  0.0 0.8 %copy-done = bf16[15,2048]{1,0:T(8,128)(2,1)S(1)} copy-done((bf16[15,2048]{1,0:T(8,128)(2,1)S(1)}, bf16[15,2048]{1,0:T(8,128)(2,1)}, u32[]{:S(2)}) %copy-start) | copy-done | bytes 61464
  0.8 0.0 copy-start.1
  0.8 0.7 %copy-done.1 = s32[16,6]{0,1:T(8,128)S(1)} copy-done((s32[16,6]{0,1:T(8,128)S(1)}, s32[16,6]{0,1:T(8,128)}, u32[]{:S(2)}) %copy-start.1) | copy-done | bytes 408
  1.5 0.0 copy-start.2
  1.5 0.7 %copy-done.2 = s32[16]{0:T(128)S(1)} copy-done((s32[16]{0:T(128)S(1)}, s32[16]{0:T(128)}, u32[]{:S(2)}) %copy-start.2) | copy-done | bytes 88
  2.2 45.4 %shard_map.46 = (bf16[4,4,6,128,128]{4,3,2,1,0:T(8,128)(2,1)S(1)}, bf16[480,768]{1,0:T(8,128)(2,1)S(1)}) custom-call(bf16[4,4,6,128,128]{4,3,2,1,0:T(8,128)(2,1)} %bitcast.6, bf16[15,2048]{1,0:T(8,128)(2,1)S(1)} %copy-done, s32[6,16]{1,0:T(8,128)S(1)} %bitcast.5, s32[16]{0:T(128)S(1)} %copy-done.2), custom_call_target="tpu_custom_call" | custom-call | tf_op jit(solution)/shard_map/pallas_call | solution.py:281
  47.5 3.3 %shard_map.47 = bf16[16,480,128]{2,1,0:T(8,128)(2,1)} custom-call(bf16[16,6,128,128]{3,2,1,0:T(8,128)(2,1)S(1)} %bitcast.4, bf16[480,768]{1,0:T(8,128)(2,1)S(1)} %get-tuple-element.8.weights), custom_call_target="tpu_custom_call" | custom-call | tf_op jit(solution)/shard_map/pallas_call | solution.py:312
Async XLA Ops:
  0.0 0.8 %copy-start = (bf16[15,2048]{1,0:T(8,128)(2,1)S(1)}, bf16[15,2048]{1,0:T(8,128)(2,1)}, u32[]{:S(2)}) copy-start(bf16[15,2048]{1,0:T(8,128)(2,1)} %panel.1) | copy-start | bytes 184324
  0.8 0.7 %copy-start.1 = (s32[16,6]{0,1:T(8,128)S(1)}, s32[16,6]{0,1:T(8,128)}, u32[]{:S(2)}) copy-start(s32[16,6]{0,1:T(8,128)} %param.6) | copy-start | bytes 1156
  1.5 0.7 %copy-start.2 = (s32[16]{0:T(128)S(1)}, s32[16]{0:T(128)}, u32[]{:S(2)}) copy-start(s32[16]{0:T(128)} %cnt_in.1) | copy-start | bytes 196

commit v4 on v3

v4 whole, which is shorter than its diff:
```python
import jax
import jax.numpy as jnp
from jax import lax
from jax.experimental import pallas as pl
from jax.experimental.pallas import tpu as pltpu
from jax.sharding import PartitionSpec as P

MESH = pl.DeviceIdType.MESH
SIDE = 4
DEPTH = 16
FAR = DEPTH // 2
ATOMS = 16
SLOTS = 6
BS = 128
PANEL = 15
SHARD = 16
PAIR = 2 * SHARD
NOCC = 480
WIDE = SLOTS * BS
PARTS = 2
NU = ATOMS // PARTS
HALF = SLOTS // 2
GROUP = 4
CHUNKS = HALF
NEXT = ((1, 0), (-1, 0), (1, 1), (-1, 1))
CHIPS = [(0, 0)] + [(q, d) for d in range(1, FAR + 1) for q in ((0, 1) if d < FAR else (0,))]
BATCH = 4
BATCHES = DEPTH // BATCH


def exchange(
    ints, panel, nbr_in, cnt_in, fin, weights,
    g0, g1, g2, g3,
    nbr, cnt, rows, mid, w32, w16,
    ready, ring_s, ring_r, sib_s, sib_r, one_s, one_r, two_s, two_r, local,
):
    batches = [g0, g1, g2, g3]
    row = lax.axis_index("row")
    col = lax.axis_index("col")
    x, y = row // SIDE, row % SIDE
    z, core = col // 2, col % 2

    def plane(dz):
        return (z + dz + DEPTH) % DEPTH

    def at(dx=0, dy=0, dz=0, dc=0):
        return (
            ((x + dx) % SIDE) * SIDE + (y + dy) % SIDE,
            plane(dz) * 2 + (core + dc) % 2,
        )

    earlier = [plane(o) < z for o, _ in NEXT]
    partners = [at(dx=d) for d in (1, 2, 3)] + [at(dy=d) for d in (1, 2, 3)] + [at(dc=1)]
    barrier = pltpu.get_barrier_semaphore()
    for p in partners:
        pl.semaphore_signal(barrier, inc=1, device_id=p, device_id_type=MESH)
    for i, (o, c) in enumerate(NEXT):

        @pl.when(jnp.logical_not(earlier[i]))
        def _():
            pl.semaphore_signal(barrier, inc=1, device_id=at(dz=o, dc=c), device_id_type=MESH)

    load = pltpu.make_async_copy(panel, rows, local.at[0])
    load.start()
    tables = [
        pltpu.make_async_copy(nbr_in, nbr, local.at[1]),
        pltpu.make_async_copy(cnt_in, cnt, local.at[2]),
    ]
    for cp in tables:
        cp.start()

    def source(h, c, d):
        if h == 0:
            return ints.at[(x + d) % SIDE, :, c]
        return ints.at[:, (y + d) % SIDE, HALF + c]

    def landing(h, c):
        return mid.at[h, c, x if h == 0 else y]

    own = []
    for c in range(CHUNKS):
        for h in range(2):
            cp = pltpu.make_async_copy(
                source(h, c, 0), landing(h, c), local.at[3 + h * CHUNKS + c]
            )
            cp.start()
            own.append(cp)
    load.wait()
    for nu in range(ATOMS):
        g0[nu, pl.ds(0, SHARD), :] = jnp.concatenate(
            [rows[:, nu * BS : (nu + 1) * BS], jnp.zeros((1, BS), jnp.bfloat16)], axis=0
        )
    w32[...] = jnp.zeros_like(w32)
    expected = len(partners)
    for e in earlier:
        expected = expected + e.astype(jnp.int32)
    pl.semaphore_wait(barrier, expected)
    for i, (o, c) in enumerate(NEXT):

        @pl.when(earlier[i])
        def _():
            pl.semaphore_signal(
                ready.at[i ^ 1], inc=1, device_id=at(dz=o, dc=c), device_id_type=MESH
            )

    def shard(q, d, mine, nus):
        n = CHIPS.index((q if 0 < d < FAR else 0, d))
        first = (n % BATCH) * PAIR + (0 if mine else SHARD)
        return batches[n // BATCH].at[nus, pl.ds(first, SHARD), :]

    def ring(q, d, p):
        nus = pl.ds(p * NU, NU)
        return pltpu.make_async_remote_copy(
            src_ref=shard(q, d - 1, True, nus),
            dst_ref=shard(q, d, True, nus),
            send_sem=ring_s.at[d, q, p],
            recv_sem=ring_r.at[d, q, p],
            device_id=at(dz=1 if q == 0 else -1),
            device_id_type=MESH,
        )

    def cross(q):
        nus = pl.ds(q * NU, NU)
        return pltpu.make_async_remote_copy(
            src_ref=shard(q, FAR - 1, True, nus),
            dst_ref=shard(q, FAR, False, nus),
            send_sem=ring_s.at[0, q, 0],
            recv_sem=ring_r.at[0, q, 0],
            device_id=at(dz=1 if q == 0 else -1, dc=1),
            device_id_type=MESH,
        )

    def moves(q, d, p):
        return d < FAR or q == p

    def sib(q, d):
        return pltpu.make_async_remote_copy(
            src_ref=shard(q, d, True, pl.ds(0, ATOMS)),
            dst_ref=shard(q, d, False, pl.ds(0, ATOMS)),
            send_sem=sib_s.at[d, q],
            recv_sem=sib_r.at[d, q],
            device_id=at(dc=1),
            device_id_type=MESH,
        )

    def first(h, c, d):
        return pltpu.make_async_remote_copy(
            src_ref=source(h, c, d),
            dst_ref=landing(h, c),
            send_sem=one_s.at[h, c, d],
            recv_sem=one_r.at[h, c, d],
            device_id=at(dx=d) if h == 0 else at(dy=d),
            device_id_type=MESH,
        )

    def held(h, c, e):
        return mid.at[h, c, :, (y + e) % SIDE if h == 0 else (x + e) % SIDE]

    def final(h, c):
        return fin.at[:, y, c] if h == 0 else fin.at[x, :, HALF + c]

    def second(h, c, e):
        return pltpu.make_async_remote_copy(
            src_ref=held(h, c, e),
            dst_ref=final(h, c),
            send_sem=two_s.at[h, c, e],
            recv_sem=two_r.at[h, c, e],
            device_id=at(dy=e) if h == 0 else at(dx=e),
            device_id_type=MESH,
        )

    def keep(h, c):
        return pltpu.make_async_copy(
            held(h, c, 0), final(h, c), local.at[3 + (2 + h) * CHUNKS + c]
        )

    def step(d):
        for p in range(PARTS):
            for q in range(2):
                if moves(q, d, p):
                    ring(q, d, p).wait_recv()
                    if d < FAR and moves(q, d + 1, p):
                        ring(q, d + 1, p).start()
                        if d + 1 == FAR:
                            cross(q).start()
        for q in range(2):
            if d < FAR:
                sib(q, d).start()
            else:
                cross(q).wait_recv()

    def forward(c):
        for h in range(2):
            own[c * 2 + h].wait()
            for d in (1, 3, 2):
                first(h, c, d).wait_recv()
            for e in (1, 3, 2):
                second(h, c, e).start()
            keep(h, c).start()

    def weigh(b):
        chips = CHIPS[b * BATCH : (b + 1) * BATCH]
        for q, d in chips:
            if d < FAR:
                sib(q, d).wait_recv()
        at_row = lax.broadcasted_iota(jnp.int32, (NOCC, BATCH * PAIR), 0)
        lane = lax.broadcasted_iota(jnp.int32, (1, BATCH * PAIR), 1)
        chip, within = lane // PAIR, lane % PAIR
        from_z = jnp.zeros_like(lane)
        for n, (q, d) in enumerate(chips):
            from_z = jnp.where(chip == n, plane(-d if q == 0 else d), from_z)
        from_core = jnp.where(within < SHARD, core, 1 - core)
        j = within % SHARD
        to_row = jnp.where(j < PANEL, (from_z * 2 + from_core) * PANEL + j, -1)
        place = (to_row == at_row).astype(jnp.float32).astype(jnp.bfloat16)
        parts = []
        for k in range(SLOTS):
            g = batches[b][nbr[k, row]]
            parts.append(jnp.where(k < cnt[row], g, jnp.zeros_like(g)))
        total = w32[...] + jnp.dot(
            place, jnp.concatenate(parts, axis=1), preferred_element_type=jnp.float32
        )
        if b + 1 < BATCHES:
            w32[...] = total
        else:
            w16[...] = total.astype(jnp.bfloat16)

    def depart(i):
        for p in range(PARTS):
            ring(i, 1, p).start()

    for c in range(CHUNKS):
        for d in (1, 3, 2):
            for h in range(2):
                first(h, c, d).start()
    sib(0, 0).start()
    for i in range(2):

        @pl.when(earlier[i])
        def _():
            depart(i)

    def depart_later(i):
        @pl.when(jnp.logical_not(earlier[i]))
        def _():
            pl.semaphore_wait(ready.at[i], 1)
            depart(i)

    depart_later(0)
    depart_later(1)
    for cp in tables:
        cp.wait()
    step(1)
    step(2)
    step(3)
    forward(0)
    step(4)
    forward(1)
    weigh(0)
    step(5)
    forward(2)
    weigh(1)
    step(6)
    for i in (2, 3):

        @pl.when(jnp.logical_not(earlier[i]))
        def _():
            pl.semaphore_wait(ready.at[i], 1)

    step(7)
    weigh(2)
    step(8)
    weigh(3)
    save = pltpu.make_async_copy(w16, weights, local.at[0])
    save.start()

    for h in range(2):
        for c in range(CHUNKS):
            keep(h, c).wait()
            for d in (1, 3, 2):
                first(h, c, d).wait_send()
                second(h, c, d).wait_send()
                second(h, c, d).wait_recv()
    for d in range(1, FAR + 1):
        for q in range(2):
            for p in range(PARTS):
                if moves(q, d, p):
                    ring(q, d, p).wait_send()
    for q, d in CHIPS:
        if d < FAR:
            sib(q, d).wait_send()
        else:
            cross(0).wait_send()
            cross(1).wait_send()
    save.wait()


def contract(blocks, weights, out, fin, w, obuf, sems):
    def fetch(g):
        group = pl.ds(g * GROUP, GROUP)
        return pltpu.make_async_copy(blocks.at[group], fin.at[group], sems.at[g])

    def store(g):
        group = pl.ds(g * GROUP, GROUP)
        return pltpu.make_async_copy(obuf.at[group], out.at[group], sems.at[groups + g])

    groups = ATOMS // GROUP
    load = pltpu.make_async_copy(weights, w, sems.at[2 * groups])
    load.start()
    for g in range(groups):
        fetch(g).start()
    load.wait()
    for g in range(groups):
        fetch(g).wait()
        rhs = [
            fin[g * GROUP : (g + 1) * GROUP, k].reshape(GROUP * BS, BS) for k in range(SLOTS)
        ]
        res = lax.dot_general(
            w[...], jnp.concatenate(rhs, axis=1), (((1,), (1,)), ((), ())),
            preferred_element_type=jnp.float32,
        )
        for p in range(GROUP):
            obuf[g * GROUP + p] = res[:, p * BS : (p + 1) * BS].astype(jnp.bfloat16)
        store(g).start()
    for g in range(groups):
        store(g).wait()


def per_device(integrals, green_panel, neighbours, slot_counts):
    blocks = integrals.reshape(SIDE, SIDE, SLOTS, BS, BS)
    anywhere = pl.BlockSpec(memory_space=pl.ANY)
    bf16, f32 = jnp.bfloat16, jnp.float32
    dma = pltpu.SemaphoreType.DMA
    gathered, weights = pl.pallas_call(
        exchange,
        out_shape=[
            jax.ShapeDtypeStruct((SIDE, SIDE, SLOTS, BS, BS), bf16),
            jax.ShapeDtypeStruct((NOCC, WIDE), bf16),
        ],
        in_specs=[anywhere] * 4,
        out_specs=[anywhere] * 2,
        scratch_shapes=[pltpu.VMEM((ATOMS, BATCH * PAIR, BS), bf16)] * BATCHES
        + [
            pltpu.SMEM((SLOTS, ATOMS), jnp.int32),
            pltpu.SMEM((ATOMS,), jnp.int32),
            pltpu.VMEM((PANEL, ATOMS * BS), bf16),
            pltpu.VMEM((2, CHUNKS, SIDE, SIDE, BS, BS), bf16),
            pltpu.VMEM((NOCC, WIDE), f32),
            pltpu.VMEM((NOCC, WIDE), bf16),
            pltpu.SemaphoreType.REGULAR((4,)),
            dma((FAR + 1, 2, PARTS)),
            dma((FAR + 1, 2, PARTS)),
            dma((FAR + 1, 2)),
            dma((FAR + 1, 2)),
            dma((2, CHUNKS, SIDE)),
            dma((2, CHUNKS, SIDE)),
            dma((2, CHUNKS, SIDE)),
            dma((2, CHUNKS, SIDE)),
            dma((3 + 4 * CHUNKS,)),
        ],
        compiler_params=pltpu.CompilerParams(
            collective_id=0, has_side_effects=True, vmem_limit_bytes=60 << 20
        ),
    )(blocks, green_panel, neighbours.T, slot_counts)
    result = pl.pallas_call(
        contract,
        out_shape=jax.ShapeDtypeStruct((ATOMS, NOCC, BS), bf16),
        in_specs=[anywhere] * 2,
        out_specs=anywhere,
        scratch_shapes=[
            pltpu.VMEM((ATOMS, SLOTS, BS, BS), bf16),
            pltpu.VMEM((NOCC, WIDE), bf16),
            pltpu.VMEM((ATOMS, NOCC, BS), bf16),
            dma((2 * ATOMS // GROUP + 1,)),
        ],
        compiler_params=pltpu.CompilerParams(vmem_limit_bytes=60 << 20),
    )(gathered.reshape(ATOMS, SLOTS, BS, BS), weights)
    return jnp.swapaxes(result, 1, 2)


def solution(mesh):
    return jax.shard_map(
        per_device,
        mesh=mesh,
        in_specs=(P(("col", "row"), None, None, None, None), P("col", None), P(), P()),
        out_specs=P("col", "row", None),
        check_vma=False,
    )
```

time: 51.1 us -> 50.1 us (0.980)
  local copies, waits for them, and re-layouts: 2.18 us -> 0 us
  Pallas kernels: 48.7 us -> 49.9 us
    unnamed x6 -> x0, local copies, waits for them, and re-layouts: 2.18 us -> none
    pallas_call x1, Pallas kernels: 3.34 us -> 4.54 us  [per_device(): pl.pallas_call(contract, out_shape=jax.ShapeDtypeStruct((ATOMS, NOCC, BS)...]
where the time goes in v4:
time: 50.1 us; the launch traced here: 49.9 us
  Pallas kernels  49.9 us (100%)
    pallas_call x1, Pallas kernels, per_device(): pl.pallas_call(exchange, out_shape=[jax.ShapeDtypeStruct((SIDE, SIDE, SLO...  45.4 us
    pallas_call x1, Pallas kernels, per_device(): pl.pallas_call(contract, out_shape=jax.ShapeDtypeStruct((ATOMS, NOCC, BS)...  4.54 us

profile of v4, /device:TPU:1, one launch (start us, length us, event | category | flops | bytes accessed | tf_op | source)
XLA Modules:
  0.0 49.9 jit_solution(9392796912955472305)
XLA Ops:
  0.0 45.4 %shard_map.46 = (bf16[4,4,6,128,128]{4,3,2,1,0:T(8,128)(2,1)}, bf16[480,768]{1,0:T(8,128)(2,1)}) custom-call(bf16[4,4,6,128,128]{4,3,2,1,0:T(8,128)(2,1)} %bitcast.5, bf16[15,2048]{1,0:T(8,128)(2,1)} %panel.1, s32[6,16]{1,0:T(8,128)} %bitcast.6, s32[16]{0:T(128)} %cnt_in.1), custom_call_target="tpu_custom_call" | custom-call | tf_op jit(solution)/shard_map/pallas_call | solution.py:334
  45.4 4.5 %shard_map.47 = bf16[16,480,128]{2,1,0:T(8,128)(2,1)} custom-call(bf16[16,6,128,128]{3,2,1,0:T(8,128)(2,1)} %bitcast.4, bf16[480,768]{1,0:T(8,128)(2,1)} %get-tuple-element.8.weights), custom_call_target="tpu_custom_call" | custom-call | tf_op jit(solution)/shard_map/pallas_call | solution.py:365

commit v5 on v4

--- a/solution.py
+++ b/solution.py
@@ -29,9 +29,9 @@
 
 
 def exchange(
-    ints, panel, nbr_in, cnt_in, fin, weights,
+    ints, panel, nbr_in, cnt_in, fin, weights, last_place, last_rows,
     g0, g1, g2, g3,
-    nbr, cnt, rows, mid, w32, w16,
+    nbr, cnt, rows, mid, w16, where_to, chosen,
     ready, ring_s, ring_r, sib_s, sib_r, one_s, one_r, two_s, two_r, local,
 ):
     batches = [g0, g1, g2, g3]
@@ -90,7 +90,6 @@
         g0[nu, pl.ds(0, SHARD), :] = jnp.concatenate(
             [rows[:, nu * BS : (nu + 1) * BS], jnp.zeros((1, BS), jnp.bfloat16)], axis=0
         )
-    w32[...] = jnp.zeros_like(w32)
     expected = len(partners)
     for e in earlier:
         expected = expected + e.astype(jnp.int32)
@@ -198,32 +197,35 @@
                 second(h, c, e).start()
             keep(h, c).start()
 
-    def weigh(b):
-        chips = CHIPS[b * BATCH : (b + 1) * BATCH]
-        for q, d in chips:
-            if d < FAR:
-                sib(q, d).wait_recv()
+    def place(b):
         at_row = lax.broadcasted_iota(jnp.int32, (NOCC, BATCH * PAIR), 0)
         lane = lax.broadcasted_iota(jnp.int32, (1, BATCH * PAIR), 1)
         chip, within = lane // PAIR, lane % PAIR
         from_z = jnp.zeros_like(lane)
-        for n, (q, d) in enumerate(chips):
+        for n, (q, d) in enumerate(CHIPS[b * BATCH : (b + 1) * BATCH]):
             from_z = jnp.where(chip == n, plane(-d if q == 0 else d), from_z)
         from_core = jnp.where(within < SHARD, core, 1 - core)
         j = within % SHARD
         to_row = jnp.where(j < PANEL, (from_z * 2 + from_core) * PANEL + j, -1)
-        place = (to_row == at_row).astype(jnp.float32).astype(jnp.bfloat16)
+        return (to_row == at_row).astype(jnp.float32).astype(jnp.bfloat16)
+
+    def choose(b):
+        for q, d in CHIPS[b * BATCH : (b + 1) * BATCH]:
+            if d < FAR:
+                sib(q, d).wait_recv()
         parts = []
         for k in range(SLOTS):
             g = batches[b][nbr[k, row]]
             parts.append(jnp.where(k < cnt[row], g, jnp.zeros_like(g)))
-        total = w32[...] + jnp.dot(
-            place, jnp.concatenate(parts, axis=1), preferred_element_type=jnp.float32
-        )
-        if b + 1 < BATCHES:
-            w32[...] = total
+        return jnp.concatenate(parts, axis=1)
+
+    def weigh(b):
+        part = jnp.dot(place(b), choose(b), preferred_element_type=jnp.float32)
+        part = part.astype(jnp.bfloat16)
+        if b == 0:
+            w16[...] = part
         else:
-            w16[...] = total.astype(jnp.bfloat16)
+            w16[...] += part
 
     def depart(i):
         for p in range(PARTS):
@@ -250,6 +252,9 @@
     depart_later(1)
     for cp in tables:
         cp.wait()
+    where_to[...] = place(BATCHES - 1)
+    save_place = pltpu.make_async_copy(where_to, last_place, local.at[2])
+    save_place.start()
     step(1)
     step(2)
     step(3)
@@ -269,11 +274,12 @@
 
     step(7)
     weigh(2)
-    step(8)
-    weigh(3)
     save = pltpu.make_async_copy(w16, weights, local.at[0])
     save.start()
-
+    step(8)
+    chosen[...] = choose(BATCHES - 1)
+    save_rows = pltpu.make_async_copy(chosen, last_rows, local.at[1])
+    save_rows.start()
     for h in range(2):
         for c in range(CHUNKS):
             keep(h, c).wait()
@@ -293,9 +299,13 @@
             cross(0).wait_send()
             cross(1).wait_send()
     save.wait()
-
-
-def contract(blocks, weights, out, fin, w, obuf, sems):
+    save_place.wait()
+    save_rows.wait()
+
+
+def contract(
+    blocks, weights, last_place, last_rows, out, fin, w, where_to, chosen, obuf, sems
+):
     def fetch(g):
         group = pl.ds(g * GROUP, GROUP)
         return pltpu.make_async_copy(blocks.at[group], fin.at[group], sems.at[g])
@@ -305,11 +315,19 @@
         return pltpu.make_async_copy(obuf.at[group], out.at[group], sems.at[groups + g])
 
     groups = ATOMS // GROUP
-    load = pltpu.make_async_copy(weights, w, sems.at[2 * groups])
-    load.start()
+    loads = [
+        pltpu.make_async_copy(weights, w, sems.at[2 * groups]),
+        pltpu.make_async_copy(last_place, where_to, sems.at[2 * groups + 1]),
+        pltpu.make_async_copy(last_rows, chosen, sems.at[2 * groups + 2]),
+    ]
+    for cp in loads:
+        cp.start()
     for g in range(groups):
         fetch(g).start()
-    load.wait()
+    for cp in loads:
+        cp.wait()
+    last = jnp.dot(where_to[...], chosen[...], preferred_element_type=jnp.float32)
+    w[...] += last.astype(jnp.bfloat16)
     for g in range(groups):
         fetch(g).wait()
         rhs = [
@@ -329,24 +347,27 @@
 def per_device(integrals, green_panel, neighbours, slot_counts):
     blocks = integrals.reshape(SIDE, SIDE, SLOTS, BS, BS)
     anywhere = pl.BlockSpec(memory_space=pl.ANY)
-    bf16, f32 = jnp.bfloat16, jnp.float32
+    bf16 = jnp.bfloat16
     dma = pltpu.SemaphoreType.DMA
-    gathered, weights = pl.pallas_call(
+    gathered, weights, last_place, last_rows = pl.pallas_call(
         exchange,
         out_shape=[
             jax.ShapeDtypeStruct((SIDE, SIDE, SLOTS, BS, BS), bf16),
             jax.ShapeDtypeStruct((NOCC, WIDE), bf16),
+            jax.ShapeDtypeStruct((NOCC, BATCH * PAIR), bf16),
+            jax.ShapeDtypeStruct((BATCH * PAIR, WIDE), bf16),
         ],
         in_specs=[anywhere] * 4,
-        out_specs=[anywhere] * 2,
+        out_specs=[anywhere] * 4,
         scratch_shapes=[pltpu.VMEM((ATOMS, BATCH * PAIR, BS), bf16)] * BATCHES
         + [
             pltpu.SMEM((SLOTS, ATOMS), jnp.int32),
             pltpu.SMEM((ATOMS,), jnp.int32),
             pltpu.VMEM((PANEL, ATOMS * BS), bf16),
             pltpu.VMEM((2, CHUNKS, SIDE, SIDE, BS, BS), bf16),
-            pltpu.VMEM((NOCC, WIDE), f32),
             pltpu.VMEM((NOCC, WIDE), bf16),
+            pltpu.VMEM((NOCC, BATCH * PAIR), bf16),
+            pltpu.VMEM((BATCH * PAIR, WIDE), bf16),
             pltpu.SemaphoreType.REGULAR((4,)),
             dma((FAR + 1, 2, PARTS)),
             dma((FAR + 1, 2, PARTS)),
@@ -365,16 +386,18 @@
     result = pl.pallas_call(
         contract,
         out_shape=jax.ShapeDtypeStruct((ATOMS, NOCC, BS), bf16),
-        in_specs=[anywhere] * 2,
+        in_specs=[anywhere] * 4,
         out_specs=anywhere,
         scratch_shapes=[
             pltpu.VMEM((ATOMS, SLOTS, BS, BS), bf16),
             pltpu.VMEM((NOCC, WIDE), bf16),
+            pltpu.VMEM((NOCC, BATCH * PAIR), bf16),
+            pltpu.VMEM((BATCH * PAIR, WIDE), bf16),
             pltpu.VMEM((ATOMS, NOCC, BS), bf16),
-            dma((2 * ATOMS // GROUP + 1,)),
+            dma((2 * ATOMS // GROUP + 3,)),
         ],
         compiler_params=pltpu.CompilerParams(vmem_limit_bytes=60 << 20),
-    )(gathered.reshape(ATOMS, SLOTS, BS, BS), weights)
+    )(gathered.reshape(ATOMS, SLOTS, BS, BS), weights, last_place, last_rows)
     return jnp.swapaxes(result, 1, 2)
 
 

time: 50.1 us -> 49.7 us (level)
    pallas_call x1, Pallas kernels: 45.4 us -> 44.9 us  [per_device(): pl.pallas_call(exchange, out_shape=[jax.ShapeDtypeStruct((SIDE, SIDE, SLO...]
where the time goes in v5:
time: 49.7 us; the launch traced here: 49.6 us
  Pallas kernels  49.6 us (100%)
    pallas_call x1, Pallas kernels, per_device(): pl.pallas_call(exchange, out_shape=[jax.ShapeDtypeStruct((SIDE, SIDE, SLO...  44.9 us
    pallas_call x1, Pallas kernels, per_device(): pl.pallas_call(contract, out_shape=jax.ShapeDtypeStruct((ATOMS, NOCC, BS)...  4.73 us

profile of v5, /device:TPU:1, one launch (start us, length us, event | category | flops | bytes accessed | tf_op | source)
XLA Modules:
  0.0 49.6 jit_solution(1802055687873910410)
XLA Ops:
  0.0 44.9 %shard_map.46 = (bf16[4,4,6,128,128]{4,3,2,1,0:T(8,128)(2,1)}, bf16[480,768]{1,0:T(8,128)(2,1)}, bf16[480,128]{1,0:T(8,128)(2,1)}, bf16[128,768]{1,0:T(8,128)(2,1)}) custom-call(bf16[4,4,6,128,128]{4,3,2,1,0:T(8,128)(2,1)} %bitcast.5, bf16[15,2048]{1,0:T(8,128)(2,1)} %panel.1, s32[6,16]{1,0:T(8,128)} %bitcast.6, s32[16]{0:T(128)} %cnt_in.1), custom_call_target="tpu_custom_call" | custom-call | tf_op jit(solution)/shard_map/pallas_call | solution.py:352
  44.9 4.7 %shard_map.47 = bf16[16,480,128]{2,1,0:T(8,128)(2,1)} custom-call(bf16[16,6,128,128]{3,2,1,0:T(8,128)(2,1)} %bitcast.4, bf16[480,768]{1,0:T(8,128)(2,1)} %get-tuple-element.10.weights, bf16[480,128]{1,0:T(8,128)(2,1)} %get-tuple-element.11.last_place, bf16[128,768]{1,0:T(8,128)(2,1)} %get-tuple-element.12.last_rows), custom_call_target="tpu_custom_call" | custom-call | tf_op jit(solution)/shard_map/pallas_call | solution.py:386

commit v6 on v5

--- a/solution.py
+++ b/solution.py
@@ -260,12 +260,10 @@
     step(3)
     forward(0)
     step(4)
+    step(5)
     forward(1)
-    weigh(0)
-    step(5)
+    step(6)
     forward(2)
-    weigh(1)
-    step(6)
     for i in (2, 3):
 
         @pl.when(jnp.logical_not(earlier[i]))
@@ -273,6 +271,8 @@
             pl.semaphore_wait(ready.at[i], 1)
 
     step(7)
+    weigh(0)
+    weigh(1)
     weigh(2)
     save = pltpu.make_async_copy(w16, weights, local.at[0])
     save.start()

time: 49.7 us -> 49 us (0.986); the launches traced: 49.6 us -> 48.2 us
  Pallas kernels: 49.6 us -> 48.2 us
    pallas_call x1, Pallas kernels: 44.9 us -> 43.5 us  [per_device(): pl.pallas_call(exchange, out_shape=[jax.ShapeDtypeStruct((SIDE, SIDE, SLO...]
where the time goes in v6:
time: 49 us; the launch traced here: 48.2 us
  Pallas kernels  48.2 us (98%)
    pallas_call x1, Pallas kernels, per_device(): pl.pallas_call(exchange, out_shape=[jax.ShapeDtypeStruct((SIDE, SIDE, SLO...  43.5 us
    pallas_call x1, Pallas kernels, per_device(): pl.pallas_call(contract, out_shape=jax.ShapeDtypeStruct((ATOMS, NOCC, BS)...  4.72 us

profile of v6, /device:TPU:1, one launch (start us, length us, event | category | flops | bytes accessed | tf_op | source)
XLA Modules:
  0.0 48.2 jit_solution(9327924482288121833)
XLA Ops:
  0.0 43.5 %shard_map.46 = (bf16[4,4,6,128,128]{4,3,2,1,0:T(8,128)(2,1)}, bf16[480,768]{1,0:T(8,128)(2,1)}, bf16[480,128]{1,0:T(8,128)(2,1)}, bf16[128,768]{1,0:T(8,128)(2,1)}) custom-call(bf16[4,4,6,128,128]{4,3,2,1,0:T(8,128)(2,1)} %bitcast.5, bf16[15,2048]{1,0:T(8,128)(2,1)} %panel.1, s32[6,16]{1,0:T(8,128)} %bitcast.6, s32[16]{0:T(128)} %cnt_in.1), custom_call_target="tpu_custom_call" | custom-call | tf_op jit(solution)/shard_map/pallas_call | solution.py:352
  43.5 4.7 %shard_map.47 = bf16[16,480,128]{2,1,0:T(8,128)(2,1)} custom-call(bf16[16,6,128,128]{3,2,1,0:T(8,128)(2,1)} %bitcast.4, bf16[480,768]{1,0:T(8,128)(2,1)} %get-tuple-element.10.weights, bf16[480,128]{1,0:T(8,128)(2,1)} %get-tuple-element.11.last_place, bf16[128,768]{1,0:T(8,128)(2,1)} %get-tuple-element.12.last_rows), custom_call_target="tpu_custom_call" | custom-call | tf_op jit(solution)/shard_map/pallas_call | solution.py:386

commit v7 on v6

--- a/solution.py
+++ b/solution.py
@@ -231,16 +231,21 @@
         for p in range(PARTS):
             ring(i, 1, p).start()
 
-    for c in range(CHUNKS):
+    def set_out(c):
         for d in (1, 3, 2):
             for h in range(2):
                 first(h, c, d).start()
-    sib(0, 0).start()
+
+    set_out(0)
     for i in range(2):
 
         @pl.when(earlier[i])
         def _():
             depart(i)
+
+    for c in range(1, CHUNKS):
+        set_out(c)
+    sib(0, 0).start()
 
     def depart_later(i):
         @pl.when(jnp.logical_not(earlier[i]))

time: 49 us -> 49 us (level)
  no operation moved by 1% of the time
where the time goes in v7:
time: 49 us; the launch traced here: 48.2 us
  Pallas kernels  48.2 us (98%)
    pallas_call x1, Pallas kernels, per_device(): pl.pallas_call(exchange, out_shape=[jax.ShapeDtypeStruct((SIDE, SIDE, SLO...  43.5 us
    pallas_call x1, Pallas kernels, per_device(): pl.pallas_call(contract, out_shape=jax.ShapeDtypeStruct((ATOMS, NOCC, BS)...  4.72 us

profile of v7, /device:TPU:1, one launch (start us, length us, event | category | flops | bytes accessed | tf_op | source)
XLA Modules:
  0.0 48.2 jit_solution(4843161444215323448)
XLA Ops:
  0.0 43.5 %shard_map.46 = (bf16[4,4,6,128,128]{4,3,2,1,0:T(8,128)(2,1)}, bf16[480,768]{1,0:T(8,128)(2,1)}, bf16[480,128]{1,0:T(8,128)(2,1)}, bf16[128,768]{1,0:T(8,128)(2,1)}) custom-call(bf16[4,4,6,128,128]{4,3,2,1,0:T(8,128)(2,1)} %bitcast.5, bf16[15,2048]{1,0:T(8,128)(2,1)} %panel.1, s32[6,16]{1,0:T(8,128)} %bitcast.6, s32[16]{0:T(128)} %cnt_in.1), custom_call_target="tpu_custom_call" | custom-call | tf_op jit(solution)/shard_map/pallas_call | solution.py:357
  43.5 4.7 %shard_map.47 = bf16[16,480,128]{2,1,0:T(8,128)(2,1)} custom-call(bf16[16,6,128,128]{3,2,1,0:T(8,128)(2,1)} %bitcast.4, bf16[480,768]{1,0:T(8,128)(2,1)} %get-tuple-element.10.weights, bf16[480,128]{1,0:T(8,128)(2,1)} %get-tuple-element.11.last_place, bf16[128,768]{1,0:T(8,128)(2,1)} %get-tuple-element.12.last_rows), custom_call_target="tpu_custom_call" | custom-call | tf_op jit(solution)/shard_map/pallas_call | solution.py:391
